TPU v7x, 512 devices: a whole 4x8x8 slice. The times are simulated.
512 devices in a mesh: rows: 8 (over z), cols: 8 (over y), depth: 8 (over x, core).
Axes of the slice: x: 4, y: 8, z: 8, core: 2. Of those that a mesh axis runs over, the one named last changes fastest.
Arguments:
- tokens: bfloat16 [512, 12288], P(('rows', 'cols'), 'depth'), may hold values from -6 to 6
- weight_in: bfloat16 [12288, 49152], P('depth', ('rows', 'cols')), may hold values from -0.0546875 to 0.0546875
- bias_in: float32 [49152], P(('rows', 'cols')), may hold values from -4 to 4
- weight_out: bfloat16 [49152, 12288], P(('rows', 'cols'), 'depth'), may hold values from -0.02734375 to 0.02734375
- bias_out: float32 [12288], P('depth'), may hold values from -3 to 3
Outputs:
- output: bfloat16 [512, 12288], P(('rows', 'cols'), 'depth')
All inputs are finite; a program needn't handle non-finite values.
Results may differ from a plain program's by a relative error of at most 0.0046.
Values may be sent and summed in bfloat16 or wider, within the bound.
No kernel may reach another device: no remote copies, remote signals or barrier semaphores. Data moves between devices by JAX's collectives and lax.ppermute only.
A program may use at most 64 MiB of HBM per device.

v0:
```python
import jax
import jax.numpy as jnp
from jax import lax
from jax.sharding import PartitionSpec as P


def shards(tokens, weight_in, bias_in, weight_out, bias_out):
    partial_value = jnp.dot(
        lax.all_gather(tokens, ("rows", "cols"), axis=0, tiled=True),
        weight_in,
        preferred_element_type=jnp.float32,
    )
    total = lax.psum(partial_value, "depth")
    active = jax.nn.gelu(total + bias_in, approximate=True).astype(jnp.bfloat16)
    summed = lax.psum_scatter(
        jnp.dot(active, weight_out, preferred_element_type=jnp.float32),
        ("rows", "cols"),
        scatter_dimension=0,
        tiled=True,
    )
    return (summed + bias_out).astype(jnp.bfloat16)


def solution(mesh):
    in_specs = (
        P(("rows", "cols"), "depth"),
        P("depth", ("rows", "cols")),
        P(("rows", "cols")),
        P(("rows", "cols"), "depth"),
        P("depth"),
    )
    out_specs = P(("rows", "cols"), "depth")
    return jax.shard_map(shards, mesh=mesh, in_specs=in_specs, out_specs=out_specs, check_vma=False)
```

profile of v0, /device:TPU:2, one launch (start us, length us, event | category | flops | bytes accessed | tf_op | source)
XLA Modules:
  0.0 353.3 jit_solution(1478955682102614328)
XLA Ops:
  6.5 0.0 copy-start
  6.5 0.0 all-gather.2.cloned.1.call-start
  6.5 0.7 all-gather.2.cloned.1.call-update
  7.3 0.0 all-reduce.4.cloned.1.call-start
  7.3 90.5 %all-gather.2.cloned.1.call-done = bf16[512,1536]{1,0:T(8,128)(2,1)} async-done(((bf16[8,1536]{1,0:T(8,128)(2,1)}), bf16[512,1536]{1,0:T(8,128)(2,1)}) %all-gather.2.cloned.1.call-update) | async-done | bytes 1572880 | tf_op jit(solution)/shard_map/all_gather | solution.py:9
  97.8 4.7 %fusion.20 = f32[512,768]{1,0:T(8,128)} fusion(bf16[512,1536]{1,0:T(8,128)(2,1)} %all-gather.2.cloned.1.call-done, bf16[1536,768]{1,0:T(8,128)(2,1)} %param.6), kind=kOutput, calls=%fused_computation.21 | convolution fusion | flops 1207959552 | bytes 5505024 | tf_op jit(solution)/shard_map/dot_general | solution.py:8
  102.5 0.0 copy-start.2
  102.5 0.0 all-reduce.4.cloned.1.call-update
  102.5 0.0 all-reduce.6.cloned.1.call-start
  102.6 69.5 %all-reduce.4.cloned.1.call-done = f32[512,768]{1,0:T(8,128)} async-done(((f32[512,768]{1,0:T(8,128)}), f32[512,768]{1,0:T(8,128)}) %all-reduce.4.cloned.1.call-update) | async-done | bytes 1572880 | tf_op jit(solution)/shard_map/psum | solution.py:13
  172.1 0.0 copy-done
  172.1 0.0 copy-done.2
  172.1 4.6 %fusion.8 = f32[512,1536]{1,0:T(8,128)} fusion(bf16[768,1536]{1,0:T(8,128)(2,1)S(1)} %copy-done, f32[512,768]{1,0:T(8,128)} %all-reduce.4.cloned.1.call-done, f32[768]{0:T(1024)S(1)} %copy-done.2), kind=kOutput, calls=%fused_computation.9 | convolution fusion | flops 1211891712 | bytes 7080960 | tf_op jit(solution)/shard_map/dot_general | solution.py:16
  176.7 0.0 copy-start.1
  176.7 0.0 all-reduce.6.cloned.1.call-update
  176.7 1.3 dynamic-slice
  178.6 166.8 %all-reduce.6.cloned.1.call-done = f32[512,1536]{1,0:T(8,128)} async-done(((f32[512,1536]{1,0:T(8,128)}), f32[512,1536]{1,0:T(8,128)}) %all-reduce.6.cloned.1.call-update) | async-done | bytes 3145744
  345.4 0.0 copy-done.1
  345.4 1.4 fusion.15
Async XLA Ops:
  6.5 165.5 %copy-start = (bf16[768,1536]{1,0:T(8,128)(2,1)S(1)}, bf16[768,1536]{1,0:T(8,128)(2,1)}, u32[]{:S(2)}) copy-start(bf16[768,1536]{1,0:T(8,128)(2,1)} %param.8) | copy-start | bytes 7077892
  6.5 91.3 %all-gather.2.cloned.1.call-start = ((), (), s32[]{:S(2)}) async-start(), calls=%async_computation | async-start | bytes 1597440 | tf_op jit(solution)/shard_map/all_gather | solution.py:9
  7.3 164.8 %all-reduce.4.cloned.1.call-start = ((), (), s32[]{:S(2)}) async-start(), calls=%async_computation.1 | async-start | bytes 3145728 | tf_op jit(solution)/shard_map/psum | solution.py:13
  102.5 69.6 %copy-start.2 = (f32[768]{0:T(1024)S(1)}, f32[768]{0:T(1024)}, u32[]{:S(2)}) copy-start(f32[768]{0:T(1024)} %param.7) | copy-start | bytes 9220
  102.5 242.8 %all-reduce.6.cloned.1.call-start = ((), (), s32[]{:S(2)}) async-start(), calls=%async_computation.2 | async-start | bytes 6291456
  176.7 168.7 %copy-start.1 = (f32[1536]{0:T(1024)S(1)}, f32[1536]{0:T(1024)}, u32[]{:S(2)}) copy-start(f32[1536]{0:T(1024)} %param.9) | copy-start | bytes 18436
Sparse Core Ops, SparseCore 0:
  10.4 87.4 all-gather.1
  102.6 69.3 all-reduce.3
  176.8 168.5 all-reduce.5
where the time goes:
time: 354 us; the launch traced here: 353 us
  waiting for transfers between devices  327 us (92%)
  between operations  13.8 us (4%)
  matrix products  9.27 us (3%)
    unnamed x4, waiting for transfers between devices  167 us
    all_gather x1, waiting for transfers between devices, shards(): lax.all_gather(tokens, ('rows', 'cols'), axis=0, tiled=True)  90.5 us
    psum x1, waiting for transfers between devices, shards(): total = lax.psum(partial_value, 'depth')  69.5 us
  transfers between devices with their start and end apart: 3, of which 3 were waited for; matrix products, arithmetic and copies ran while one was open for 0% of the time, Pallas kernels for 0%

commit v1 on v0

--- a/solution.py
+++ b/solution.py
@@ -6,7 +6,12 @@
 
 def shards(tokens, weight_in, bias_in, weight_out, bias_out):
     partial_value = jnp.dot(
-        lax.all_gather(tokens, ("rows", "cols"), axis=0, tiled=True),
+        jnp.concatenate(
+            lax.all_to_all(
+                jnp.stack([tokens] * lax.axis_size(("rows", "cols"))), ("rows", "cols"), 0, 0
+            ),
+            axis=0,
+        ),
         weight_in,
         preferred_element_type=jnp.float32,
     )

time: 354 us -> 318 us (0.90)
  waiting for transfers between devices: 327 us -> 235 us
  blocking collectives: 0 us -> 57.8 us
    all_gather x1 -> x0, waiting for transfers between devices: 90.5 us -> none  [shards(): lax.all_gather(tokens, ('rows', 'cols'), axis=0, tiled=True)]
    all_to_all x0 -> x1, blocking collectives: none -> 57.8 us  [shards(): lax.all_to_all(jnp.stack([tokens] * lax.axis_size(('rows', 'cols'))), ('r...]
    unnamed x4 -> x3, waiting for transfers between devices: 167 us -> 167 us
  transfers between devices with their start and end apart: 3 -> 2, of which waited for: 3 -> 2; matrix products, arithmetic and copies ran while one was open for 0% -> 0% of each run, Pallas kernels for 0% -> 0%
where the time goes in v1:
time: 318 us
  waiting for transfers between devices  235 us (74%)
  blocking collectives  57.8 us (18%)
  between operations  14.1 us (4%)
  matrix products  7.13 us (2%)
    unnamed x3, waiting for transfers between devices  167 us
    psum x1, waiting for transfers between devices, shards(): total = lax.psum(partial_value, 'depth')  68.2 us
    all_to_all x1, blocking collectives, shards(): lax.all_to_all(jnp.stack([tokens] * lax.axis_size(('rows', 'cols'))), ('r...  57.8 us
  transfers between devices with their start and end apart: 2, of which 2 were waited for; matrix products, arithmetic and copies ran while one was open for 0% of the time, Pallas kernels for 0%

profile of v1, /device:TPU:2, one launch (start us, length us, event | category | flops | bytes accessed | tf_op | source)
XLA Modules:
  0.0 317.8 jit_solution(13465338840589327875)
XLA Ops:
  6.5 0.0 copy-start
  6.5 0.0 all-reduce.4.cloned.1.call-start
  6.5 1.0 stack.2
  7.5 0.0 copy-start.2
  7.5 57.8 %all_to_all.5 = bf16[64,8,1536]{2,1,0:T(8,128)(2,1)S(1)} all-to-all(bf16[64,8,1536]{2,1,0:T(8,128)(2,1)S(1)} %stack.2), channel_id=1, replica_groups=mesh['rows'=8,'cols'=8,'depth'=8] {'rows','cols'}, dimensions={0} | all-to-all | bytes 3145728 | tf_op jit(solution)/shard_map/all_to_all | solution.py:10
  65.3 0.0 copy-done.2
  65.3 2.5 fusion.8
  67.9 0.0 copy-start.3
  67.9 0.0 all-reduce.4.cloned.1.call-update
  67.9 0.0 all-reduce.6.cloned.1.call-start
  68.0 68.2 %all-reduce.4.cloned.1.call-done = f32[512,768]{1,0:T(8,128)} async-done(((f32[512,768]{1,0:T(8,128)}), f32[512,768]{1,0:T(8,128)}) %all-reduce.4.cloned.1.call-update) | async-done | bytes 1572880 | tf_op jit(solution)/shard_map/psum | solution.py:18
  136.1 0.0 copy-done
  136.1 0.0 copy-done.3
  136.2 4.6 %fusion.10 = f32[512,1536]{1,0:T(8,128)} fusion(bf16[768,1536]{1,0:T(8,128)(2,1)S(1)} %copy-done, f32[512,768]{1,0:T(8,128)} %all-reduce.4.cloned.1.call-done, f32[768]{0:T(1024)S(1)} %copy-done.3), kind=kOutput, calls=%fused_computation.11 | convolution fusion | flops 1211891712 | bytes 7080960 | tf_op jit(solution)/shard_map/dot_general | solution.py:21
  140.7 0.0 copy-start.1
  140.7 0.0 all-reduce.6.cloned.1.call-update
  140.8 1.3 dynamic-slice
  142.7 166.8 %all-reduce.6.cloned.1.call-done = f32[512,1536]{1,0:T(8,128)} async-done(((f32[512,1536]{1,0:T(8,128)}), f32[512,1536]{1,0:T(8,128)}) %all-reduce.6.cloned.1.call-update) | async-done | bytes 3145744
  309.5 0.0 copy-done.1
  309.5 1.4 fusion.17
Async XLA Ops:
  6.5 129.6 %copy-start = (bf16[768,1536]{1,0:T(8,128)(2,1)S(1)}, bf16[768,1536]{1,0:T(8,128)(2,1)}, u32[]{:S(2)}) copy-start(bf16[768,1536]{1,0:T(8,128)(2,1)} %param.8) | copy-start | bytes 7077892
  6.5 129.6 %all-reduce.4.cloned.1.call-start = ((), (), s32[]{:S(2)}) async-start(), calls=%async_computation.1 | async-start | bytes 3145728 | tf_op jit(solution)/shard_map/psum | solution.py:18
  7.5 57.8 %copy-start.2 = (bf16[1536,768]{1,0:T(8,128)(2,1)S(1)}, bf16[1536,768]{1,0:T(8,128)(2,1)}, u32[]{:S(2)}) copy-start(bf16[1536,768]{1,0:T(8,128)(2,1)} %param.6) | copy-start | bytes 7077892
  67.9 68.3 %copy-start.3 = (f32[768]{0:T(1024)S(1)}, f32[768]{0:T(1024)}, u32[]{:S(2)}) copy-start(f32[768]{0:T(1024)} %param.7) | copy-start | bytes 9220
  67.9 241.6 %all-reduce.6.cloned.1.call-start = ((), (), s32[]{:S(2)}) async-start(), calls=%async_computation.2 | async-start | bytes 6291456
  140.7 168.8 %copy-start.1 = (f32[1536]{0:T(1024)S(1)}, f32[1536]{0:T(1024)}, u32[]{:S(2)}) copy-start(f32[1536]{0:T(1024)} %param.9) | copy-start | bytes 18436
Sparse Core Ops, SparseCore 0:
  68.0 68.0 all-reduce.3
  140.9 168.5 all-reduce.5
